TPU v7x, 32 devices: a whole 2x2x4 slice. The times are simulated.
32 devices in a mesh: row: 16 (over z, y, x), col: 2 (over core).
Axes of the slice: x: 2, y: 2, z: 4, core: 2. Of those that a mesh axis runs over, the one named last changes fastest.
Arguments:
- traces: float32 [16, 8192], P('col', 'row'), may hold values from -50 to 50
Outputs:
- overwritten: float32 [8192, 4096], P('row', 'col')
- coupling: float32 [256, 4096], P(None, 'col')
All inputs are finite; a program needn't handle non-finite values.
Results may differ from a plain program's by a relative error of at most 0.0015.
Values sent between devices are 32-bit elements; how exact they have to be, the bound alone decides.
No kernel may reach another device: no remote copies, remote signals or barrier semaphores. Data moves between devices by JAX's collectives and lax.ppermute only.
A program may use at most 64 MiB of HBM per device.

v0:
```python
import jax
import jax.numpy as jnp
from jax import lax
from jax.sharding import PartitionSpec as P

TAPS = 256
WIDE = 256


def from_behind(value, axis, steps):
    count = lax.axis_size(axis)
    leading, last = (max(0, -steps), min(count, count - steps))
    return lax.ppermute(value, axis, [(source, source + steps) for source in range(leading, last)])


def from_root(value, axis, source):
    kept = jnp.where(lax.axis_index(axis) == source, value, 0).astype(value.dtype)
    return lax.psum(kept, axis)


def hankel_piece(segment, row_count, col_count):
    length = segment.shape[-1]
    flipped = jnp.flip(segment, -1)
    repeated = jnp.tile(flipped, (1, row_count + 1))[:, : row_count * (length + 1)]
    hankel_table = repeated.reshape(segment.shape[0], row_count, length + 1)[:, :, :col_count]
    return jnp.flip(hankel_table, 1)


def toeplitz_local(extended, tap_count, col_count):
    rows_total = extended.shape[1] - tap_count
    step_rows = min(512, rows_total)
    pieces = hankel_piece(extended, step_rows, col_count)
    return pieces


def triangle_inverse(gram_part):
    factor_low = jnp.linalg.cholesky(gram_part)
    return jax.scipy.linalg.solve_triangular(
        factor_low, jnp.eye(gram_part.shape[0], dtype=jnp.float32), lower=True
    )


def body(traces):
    highest = lax.Precision.HIGHEST
    rows_here = traces.shape[1]
    total_rows = rows_here * lax.axis_size("row")
    history = from_behind(traces[:, rows_here - TAPS :], "row", 1)
    extended = jnp.concatenate([history, traces], axis=1)
    local_taps = toeplitz_local(extended, TAPS, TAPS)
    matrix = jnp.transpose(local_taps, (1, 0, 2)).reshape(rows_here, -1)
    group_cols = matrix.shape[1]
    source = from_root(extended[0:1], "col", 0)
    panel_cols = toeplitz_local(source, TAPS, WIDE)[0]
    gram_local = jnp.dot(panel_cols.T, panel_cols, precision=highest)
    cross_local = jnp.dot(panel_cols.T, matrix, precision=highest)
    gram_sum, cross_sum = lax.psum((gram_local, cross_local), "row")
    inverse = triangle_inverse(gram_sum / total_rows)
    basis_cols = jnp.dot(panel_cols, inverse.T, precision=highest)
    coupling = jnp.dot(inverse, cross_sum / total_rows, precision=highest)
    remainder = matrix - jnp.dot(basis_cols, coupling, precision=highest)
    columns = lax.axis_index("col") * group_cols + jnp.arange(group_cols)
    placed = jnp.concatenate(
        [basis_cols, jnp.zeros((rows_here, group_cols - WIDE), jnp.float32)], axis=1
    )
    overwritten = jnp.where((columns < WIDE)[None, :], placed, remainder)
    return (overwritten, coupling)


def solution(mesh):
    return jax.shard_map(
        body,
        mesh=mesh,
        in_specs=(P("col", "row"),),
        out_specs=(P("row", "col"), P(None, "col")),
        check_vma=False,
    )
```

profile of v0, /device:TPU:0, one launch (start us, length us, event | category | flops | bytes accessed | tf_op | source)
XLA Modules:
  0.0 333.4 jit_solution(10047377426847426984)
XLA Ops:
  7.9 4.8 %collective-permute-start = (f32[8,256]{1,0:T(8,128)S(1)}, f32[8,256]{1,0:T(8,128)S(1)}, u32[]{:S(2)}, u32[]{:S(2)}) collective-permute-start(f32[8,256]{1,0:T(8,128)S(1)} %slice.66), channel_id=1, source_target_pairs={{0,2},{2,4},{4,6},{6,8},{8,10},{10,12},{12,14},{14,16},{16,18},{18... | collective-permute-start | bytes 24584 | tf_op jit(solution)/shard_map/ppermute | solution.py:13
  12.8 1.3 collective-permute-done
  16.1 4.8 %slice.86 = f32[8,393728]{1,0:T(8,128)} slice(f32[8,393984]{1,0:T(8,128)S(1)} %bitcast.49), slice={[0:8], [0:393728]} | slice | bytes 25198592 | tf_op jit(solution)/shard_map/slice | solution.py:24
  20.9 10.0 %reshape.71 = f32[3149824]{0:T(1024)} reshape(f32[8,393728]{1,0:T(8,128)} %slice.86) | data formatting | bytes 25198592
  30.9 17.4 %reshape.48 = f32[8,512,769]{2,1,0:T(8,128)} reshape(f32[3149824]{0:T(1024)} %reshape.71) | data formatting | bytes 25198592 | tf_op jit(solution)/shard_map/reshape | solution.py:25
  48.3 4.5 %slice.87 = f32[8,512,256]{2,1,0:T(8,128)} slice(f32[8,512,769]{2,1,0:T(8,128)} %reshape.48), slice={[0:8], [0:512], [0:256]} | slice | bytes 8388608 | tf_op jit(solution)/shard_map/slice | solution.py:25
  52.8 32.5 %rev.19 = f32[8,512,256]{2,1,0:T(8,128)} reverse(f32[8,512,256]{2,1,0:T(8,128)} %slice.87), dimensions={1} | reverse | bytes 8388608 | tf_op jit(solution)/shard_map/jit(_flip)/rev | solution.py:26
  85.3 4.8 %copy.9 = f32[8,64,8,256]{3,2,0,1:T(8,128)} copy(f32[8,64,8,256]{3,2,1,0:T(8,128)} %bitcast.52) | data formatting | bytes 8388608 | tf_op jit(solution)/shard_map/reshape | solution.py:50
  90.7 2.5 psum.21
  93.3 1.6 copy.10
  94.9 16.2 %slice_reduce_fusion = f32[393728]{0:T(1024)S(1)} fusion(f32[1,393984]{1,0:T(1,128)S(1)} %bitcast.53), kind=kLoop, calls=%fused_computation.5 | loop fusion | bytes 3149824 | tf_op jit(solution)/shard_map/slice | solution.py:24
  111.1 1.6 reshape.47
  113.2 1.7 fusion.7
  114.9 7.1 %fusion.3 = f32[256,2048]{1,0:T(8,128)} fusion(f32[512,2048]{1,0:T(8,128)} %bitcast.50, f32[1,512,256]{2,1,0:T(8,128)S(1)} %rev.17), kind=kOutput, calls=%fused_computation.10 | convolution fusion | flops 3221225472 | bytes 6815744 | tf_op jit(solution)/shard_map/dot_general | solution.py:55
  122.2 133.5 %all-reduce.5.cloned.1.call-done = (f32[256,256]{0,1:T(8,128)}, f32[256,2048]{1,0:T(8,128)}) async-done(((f32[256,256]{0,1:T(8,128)}, f32[256,2048]{1,0:T(8,128)}), (f32[256,256]{0,1:T(8,128)}, f32[256,2048]{1,0:T(8,128)})) %all-reduce.5.cloned.1.call-update) | async-done | bytes 2359312 | tf_op jit(solution)/shard_map/psum | solution.py:56
  257.8 11.7 %cholesky.50 = f32[128,128]{1,0:T(8,128)S(1)} custom-call(f32[128,128]{1,0:T(8,128)S(1)} %cholesky.118), custom_call_target="Cholesky" | custom-call | tf_op jit(solution)/shard_map/jit(cholesky)/cholesky | solution.py:37
  269.6 9.8 %custom-call.15 = f32[1,128,128]{1,2,0:T(8,128)S(1)} custom-call(f32[1,128,128]{2,1,0:T(8,128)S(1)} %get-tuple-element.25), custom_call_target="InvertDiagBlocksLowerTriangular" | custom-call | tf_op jit(solution)/shard_map/jit(cholesky)/cholesky | solution.py:37
  279.9 12.0 %cholesky.105 = f32[128,128]{1,0:T(8,128)S(1)} custom-call(f32[128,128]{1,0:T(8,128)S(1)} %convolution_subtract_fusion.1), custom_call_target="Cholesky" | custom-call | tf_op jit(solution)/shard_map/jit(cholesky)/cholesky | solution.py:37
  293.9 3.9 %while.1 = (s32[]{:T(128)}, f32[256,256]{1,0:T(8,128)S(1)}, s32[2,2]{1,0:T(2,128)S(1)}, f32[2,128,128]{2,1,0:T(8,128)S(1)}, s32[]{:T(128)}) while((s32[]{:T(128)}, f32[256,256]{1,0:T(8,128)S(1)}, s32[2,2]{1,0:T(2,128)S(1)}, f32[2,128,128]{2,1,0:T(8,128)S(1)}, s32[]{:T(128)}) %tuple.27), condition=%wide.while_cond, body=%wide.while_body.sunk | while | flops 2 | bytes 131189 | solution.py:38
  294.5 1.4 bitcast_dynamic-update-slice_fusion.2
  296.5 1.4 bitcast_dynamic-update-slice_fusion.2
  297.9 19.7 %custom-call.16 = f32[2,128,128]{1,2,0:T(8,128)S(1)} custom-call(f32[2,128,128]{2,1,0:T(8,128)S(1)} %get-tuple-element.9), custom_call_target="InvertDiagBlocksLowerTriangular" | custom-call | tf_op jit(solution)/shard_map/jit(_solve_triangular)/triangular_solve | solution.py:38
  319.0 1.9 fusion
  321.2 5.3 %subtract_select_fusion = f32[512,2048]{1,0:T(8,128)} fusion(f32[512,2048]{1,0:T(8,128)S(1)} %bitcast.51, f32[512,256]{1,0:T(8,128)S(1)} %fusion.5, f32[256,2048]{1,0:T(8,128)S(1)} %fusion, pred[2048]{0:T(1024)(128)(4,1)S(1)} %add_compare_fusion), kind=kOutput, calls=%fused_computation.2 | convolution fusion | flops 3223322624 | bytes 11012096 | tf_op jit(solution)/shard_map/dot_general | solution.py:60
  (43 shorter events, 10.3 us)
Async XLA Ops:
  7.2 248.5 %all-reduce.5.cloned.1.call-start = ((), (), s32[]{:S(2)}) async-start(), calls=%async_computation | async-start | bytes 4718592 | tf_op jit(solution)/shard_map/psum | solution.py:56
  7.9 6.2 %collective-permute-start = (f32[8,256]{1,0:T(8,128)S(1)}, f32[8,256]{1,0:T(8,128)S(1)}, u32[]{:S(2)}, u32[]{:S(2)}) collective-permute-start(f32[8,256]{1,0:T(8,128)S(1)} %slice.66), channel_id=1, source_target_pairs={{0,2},{2,4},{4,6},{6,8},{8,10},{10,12},{12,14},{14,16},{16,18},{18... | collective-permute-start | bytes 24584 | tf_op jit(solution)/shard_map/ppermute | solution.py:13
  279.4 39.6 %copy-start.2 = (f32[256,2048]{1,0:T(8,128)S(1)}, f32[256,2048]{1,0:T(8,128)}, u32[]{:S(2)}) copy-start(f32[256,2048]{1,0:T(8,128)} %get-tuple-element.19) | copy-start | bytes 6291460
  319.0 2.2 copy-start
  321.2 5.3 %copy-start.1 = (f32[256,2048]{1,0:T(8,128)}, f32[256,2048]{1,0:T(8,128)S(1)}, u32[]{:S(2)}) copy-start(f32[256,2048]{1,0:T(8,128)S(1)} %fusion) | copy-start | bytes 6291460
Sparse Core Ops, SparseCore 0:
  122.2 133.4 all-reduce.4
where the time goes:
time: 336 us; the launch traced here: 333 us
  waiting for transfers between devices  135 us (40%)
  local copies, waits for them, and re-layouts  102 us (30%)
  other arithmetic  55.9 us (17%)
  matrix products  18 us (5%)
  between operations  15.5 us (5%)
  starting transfers between devices  4.87 us (1%)
    psum x1, waiting for transfers between devices, body(): gram_sum, cross_sum = lax.psum((gram_local, cross_local), 'row')  134 us
    another operation x6, other arithmetic, triangle_inverse(): factor_low = jnp.linalg.cholesky(gram_part)  34.2 us
    rev x2, local copies, waits for them, and re-layouts, hankel_piece(): return jnp.flip(hankel_table, 1)  33 us
    slice x2, local copies, waits for them, and re-layouts, hankel_piece(): jnp.tile(flipped, (1, row_count + 1))[:, :row_count * (length + 1)]  21 us
    another operation x3, other arithmetic, triangle_inverse(): jax.scipy.linalg.solve_triangular(factor_low, jnp.eye(gram_part.shape[0],...  19.7 us
    reshape x2, local copies, waits for them, and re-layouts, hankel_piece(): repeated.reshape(segment.shape[0], row_count, length + 1)[:, :, :col_count]  19 us
    unnamed x10, local copies, waits for them, and re-layouts  12 us
    dot_general x1, matrix products, body(): cross_local = jnp.dot(panel_cols.T, matrix, precision=highest)  7.15 us
  transfers between devices with their start and end apart: 2, of which 2 were waited for; matrix products, arithmetic and copies ran while one was open for 0% of the time, Pallas kernels for 0%

commit v1 on v0

v1 whole, which is shorter than its diff:
```python
import functools

import jax
import jax.numpy as jnp
from jax import lax
from jax.experimental import pallas as pl
from jax.experimental.pallas import tpu as pltpu
from jax.sharding import PartitionSpec as P

TAPS = 256
WIDE = 256
LANES = 128
PANEL = 32
F32 = jnp.float32
BF16 = jnp.bfloat16
LEFT = (0, 0, 1, 0, 2, 1)
RIGHT = (0, 1, 0, 2, 0, 1)
NT = (((1,), (1,)), ((), ()))
TN = (((0,), (0,)), ((), ()))


def split(x, count=3):
    pieces = []
    for _ in range(count - 1):
        pieces.append(x.astype(BF16))
        x = x - pieces[-1].astype(F32)
    pieces.append(x.astype(BF16))
    return pieces


def dot(a, b, dims=None):
    if dims is None:
        return jnp.dot(a, b, preferred_element_type=F32)
    return lax.dot_general(a, b, dims, preferred_element_type=F32)


def dot_split(a, b, dims=None):
    return dot(a[0], b[0], dims) + (dot(a[0], b[1], dims) + dot(a[1], b[0], dims))


def row_of(x, j):
    return jnp.broadcast_to(x[j : j + 1, :], x.shape)


def inverse_factor(m, n):
    sub = lax.broadcasted_iota(jnp.int32, (8, LANES), 0)
    groups = PANEL // 8
    half = n // LANES
    for r0 in range(0, n, PANEL):
        cols = list(range(r0 // LANES, half)) + [half + i for i in range((r0 + PANEL - 1) // LANES + 1)]
        v = [{c: m[r0 + 8 * g : r0 + 8 * g + 8, LANES * c : LANES * (c + 1)] for c in cols} for g in range(groups)]
        for p in range(groups):
            tile, lane = divmod(r0 + 8 * p, LANES)
            col = [
                [jnp.broadcast_to(v[g][tile][:, lane + k : lane + k + 1], (8, LANES)) if g >= p else None for g in range(groups)]
                for k in range(8)
            ]
            pivots = jnp.ones((8, LANES), F32)
            for j in range(8):
                pivot = row_of(col[j][p], j)
                pivots = jnp.where(sub == j, pivot, pivots)
                if j == 7 and p == groups - 1:
                    continue
                inv = 1.0 / pivot
                first = p if j < 7 else p + 1
                factor = {g: col[j][g] * inv for g in range(first, groups)}
                if first == p:
                    factor[p] = jnp.where(sub > j, factor[p], 0.0)
                for k in range(j + 1, 8):
                    row = row_of(col[k][p], j)
                    for g in range(first, groups):
                        col[k][g] = col[k][g] - factor[g] * row
                for c in cols:
                    row = row_of(v[p][c], j)
                    for g in range(first, groups):
                        v[g][c] = v[g][c] - factor[g] * row
            scale = lax.rsqrt(pivots)
            for c in cols:
                v[p][c] = v[p][c] * scale
        for g in range(groups):
            for c in cols:
                m[r0 + 8 * g : r0 + 8 * g + 8, LANES * c : LANES * (c + 1)] = v[g][c]
        done = r0 + PANEL
        if done < n:
            pieces = {c: split(jnp.concatenate([v[g][c] for g in range(groups)], 0)) for c in cols}
            for a in range(done // LANES, half):
                left = jnp.concatenate([pieces[a][i] for i in LEFT], 0)
                skip = max(0, done - LANES * a)
                for c in cols:
                    if c >= a:
                        right = jnp.concatenate([pieces[c][i] for i in RIGHT], 0)
                        update = dot(left, right, TN)
                        m[LANES * a + skip : LANES * (a + 1), LANES * c : LANES * (c + 1)] -= update[skip:, :]


def toeplitz(base, first, rows, store):
    width = base.shape[1]
    tiles = width // LANES
    strip = pltpu.roll(jnp.broadcast_to(base, (8, width)), first, 1, stride=1, stride_axis=0)
    for g in range(LANES // 8):
        turned = pltpu.roll(strip, 8 * g, 1) if g else strip
        for h in range(rows // LANES):
            for j in range(TAPS // LANES):
                t = (j - h) % tiles
                store(LANES * h + 8 * g, LANES * j, turned[:, LANES * t : LANES * (t + 1)])


def kernel(
    sizes, place, seen, over_out, coup_out,
    natural, lead, reverse_lead, lags, cross, gram, tail_low, tail_left, window, panel, over, coup, sems_a, sems_b,
):
    n_row, n_col, nc, rows = sizes
    per = rows // LANES
    blocks = n_row * per
    total = n_row * rows
    lag_tiles = TAPS // LANES
    my_row, my_col = place[0], place[1]

    for r in range(n_row):
        for q in range(per):
            t = r * per + q
            natural[t * nc : (t + 1) * nc, :] = seen[r * n_col + my_col, :, LANES * q : LANES * (q + 1)]
            lead[8 + t : 9 + t, :] = seen[r * n_col, 0:1, LANES * q : LANES * (q + 1)]
    lead[0:8, :] = jnp.zeros((8, LANES), F32)
    lead[8 + blocks : 16 + blocks, :] = jnp.zeros((8, LANES), F32)

    ia = lax.broadcasted_iota(jnp.int32, (LANES, LANES), 0)
    ib = lax.broadcasted_iota(jnp.int32, (LANES, LANES), 1)
    turn = (ia + ib == LANES - 1).astype(F32).astype(BF16)

    def samples(c):
        if c == nc:
            return lead[8 : 8 + blocks, :]
        return natural[pl.ds(c, blocks, stride=nc), :]

    step = lax.broadcasted_iota(jnp.int32, (blocks, LANES), 0)
    shifted = []
    for a in range(-lag_tiles, lag_tiles + 1):
        piece = lead[8 + a : 8 + a + blocks, :]
        keep = step < blocks - lag_tiles if a >= 0 else step + a < blocks - lag_tiles
        shifted.append(jnp.where(keep, piece, 0.0))
    right = split(jnp.concatenate(shifted, 1))
    right = jnp.concatenate([right[i] for i in RIGHT], 0)
    width = right.shape[1]
    for c in [nc] + list(range(nc)):
        pieces = split(samples(c))
        left = dot(turn, jnp.concatenate([pieces[i] for i in LEFT], 0), NT).astype(BF16)
        z = dot(left, right)
        parts = [z[8 * g : 8 * g + 8, :] for g in range(LANES // 8)]
        size = 8
        while len(parts) > 1:
            parts = [parts[i] + pltpu.roll(parts[i + 1], size, 1) for i in range(0, len(parts), 2)]
            size *= 2
        skewed = pltpu.roll(parts[0], 0, 1, stride=1, stride_axis=0)
        lags[c : c + 1, :] = jnp.sum(skewed, axis=0, keepdims=True)

    def put(ref, base):
        def store(i, j, tile):
            ref[i : i + 8, base + j : base + j + LANES] = tile

        return store

    zeros = jnp.zeros((1, TAPS), F32)

    def reversed_blocks(c, first, count):
        if c == nc:
            piece = lead[pl.ds(8 + first, count), :]
        else:
            piece = jnp.concatenate([natural[pl.ds((first + q) * nc + c, 1), :] for q in range(count)], 0)
        flipped = sum(dot(x, turn) for x in reversed(split(piece)))
        return jnp.concatenate([flipped[q : q + 1, :] for q in reversed(range(count))], 1)

    forward = jnp.concatenate([lead[8 + blocks - lag_tiles + q : 9 + blocks - lag_tiles + q, :] for q in range(lag_tiles)], 1)
    toeplitz(jnp.concatenate([forward, zeros], 1), 0, TAPS, put(tail_left, 0))
    left_pieces = split(tail_left[...])
    left6 = jnp.concatenate([left_pieces[i] for i in LEFT], 1)

    def crossed(c, out, base):
        toeplitz(jnp.concatenate([reversed_blocks(c, blocks - lag_tiles, lag_tiles), zeros], 1), 1 + TAPS, TAPS, put(tail_low, 0))
        toeplitz(lags[c : c + 1, :], 1 + TAPS, TAPS, put(out, base))
        pieces = split(tail_low[...])
        extra = dot(left6, jnp.concatenate([pieces[i] for i in RIGHT], 0))
        out[:, base : base + TAPS] = (out[:, base : base + TAPS] + extra) * (1.0 / total)

    crossed(nc, gram, 0)
    ga = lax.broadcasted_iota(jnp.int32, (WIDE, WIDE), 0)
    gb = lax.broadcasted_iota(jnp.int32, (WIDE, WIDE), 1)
    gram[:, WIDE:] = (ga == gb).astype(F32)
    inverse_factor(gram, WIDE)
    inverse = split(gram[:, WIDE:], 2)

    history = jnp.where(my_row > 0, 1.0, 0.0)
    start = my_row * per

    def own_rows(c, ref):
        now = reversed_blocks(c, start, per)
        before = reversed_blocks(c, jnp.maximum(start - lag_tiles, 0), lag_tiles) * history
        toeplitz(jnp.concatenate([now, before], 1), 1 + TAPS, rows, put(ref, 0))

    own_rows(nc, window)
    basis_all = dot_split(split(window[...], 2), inverse, NT)
    panel[...] = basis_all
    basis = split(basis_all, 2)

    copies = []
    for c in range(nc):
        at = pl.ds(c * TAPS, TAPS)
        crossed(c, cross, 0)
        coupling = dot_split(inverse, split(cross[...], 2))
        coup[:, at] = coupling
        copies.append(pltpu.make_async_copy(coup.at[:, at], coup_out.at[:, at], sems_a.at[c]))
        copies[-1].start()
        own_rows(c, window)
        rest = window[...] - dot_split(basis, split(coupling, 2))
        if c * TAPS < WIDE:
            rest = jnp.where(my_col == 0, panel[...], rest)
        over[:, at] = rest
        copies.append(pltpu.make_async_copy(over.at[:, at], over_out.at[:, at], sems_b.at[c]))
        copies[-1].start()
    for copy in copies:
        copy.wait()


def body(traces):
    n_row, n_col = lax.axis_size("row"), lax.axis_size("col")
    nc, rows = traces.shape
    sent = jnp.broadcast_to(traces[None], (n_row * n_col, nc, rows))
    seen = lax.all_to_all(sent, ("row", "col"), 0, 0)
    place = jnp.stack([lax.axis_index("row"), lax.axis_index("col")]).astype(jnp.int32)
    blocks = n_row * rows // LANES
    lag_tiles = TAPS // LANES
    return pl.pallas_call(
        functools.partial(kernel, (n_row, n_col, nc, rows)),
        out_shape=(
            jax.ShapeDtypeStruct((rows, nc * TAPS), F32),
            jax.ShapeDtypeStruct((WIDE, nc * TAPS), F32),
        ),
        in_specs=[pl.BlockSpec(memory_space=pltpu.SMEM), pl.BlockSpec(memory_space=pltpu.VMEM)],
        out_specs=[pl.BlockSpec(memory_space=pl.ANY)] * 2,
        scratch_shapes=[
            pltpu.VMEM((blocks * nc, LANES), F32),
            pltpu.VMEM((blocks + 16, LANES), F32),
            pltpu.VMEM((8, LANES), F32),
            pltpu.VMEM((nc + 8, (2 * lag_tiles + 1) * LANES), F32),
            pltpu.VMEM((WIDE, TAPS), F32),
            pltpu.VMEM((WIDE, 2 * WIDE), F32),
            pltpu.VMEM((TAPS, TAPS), F32),
            pltpu.VMEM((WIDE, TAPS), F32),
            pltpu.VMEM((rows, TAPS), F32),
            pltpu.VMEM((rows, WIDE), F32),
            pltpu.VMEM((rows, nc * TAPS), F32),
            pltpu.VMEM((WIDE, nc * TAPS), F32),
            pltpu.SemaphoreType.DMA((nc,)),
            pltpu.SemaphoreType.DMA((nc,)),
        ],
        compiler_params=pltpu.CompilerParams(vmem_limit_bytes=48 * 2**20),
    )(place, seen)


def solution(mesh):
    return jax.shard_map(
        body,
        mesh=mesh,
        in_specs=(P("col", "row"),),
        out_specs=(P("row", "col"), P(None, "col")),
        check_vma=False,
    )
```

time: 336 us -> 47.4 us (0.14)
  waiting for transfers between devices: 135 us -> 15.5 us
  local copies, waits for them, and re-layouts: 102 us -> 1.57 us
  other arithmetic: 55.9 us -> 0.08 us
  Pallas kernels: 0 us -> 22 us
  matrix products: 18 us -> 0 us
  between operations: 15.5 us -> 0.64 us
    psum x1 -> x0, waiting for transfers between devices: 134 us -> none  [body(): gram_sum, cross_sum = lax.psum((gram_local, cross_local), 'row')]
    another operation x9 -> x1, other arithmetic: 53.9 us -> 0.08 us  [body(): jnp.stack([lax.axis_index('row'), lax.axis_index('col')]).astype(jnp.int32)]
    rev x4 -> x0, local copies, waits for them, and re-layouts: 34 us -> none  [the longest x2 33 us: hankel_piece(): return jnp.flip(hankel_table, 1)]
    slice x5 -> x0, local copies, waits for them, and re-layouts: 26.3 us -> none  [the longest x2 21 us: hankel_piece(): jnp.tile(flipped, (1, row_count + 1))[:, :row_count * (length + 1)]]
    reshape x3 -> x0, local copies, waits for them, and re-layouts: 23.8 us -> none  [the longest x2 19 us: hankel_piece(): repeated.reshape(segment.shape[0], row_count, length + 1)[:, :, :col_count]]
    pallas_call x0 -> x1, Pallas kernels: none -> 22 us  [body(): pl.pallas_call(functools.partial(kernel, (n_row, n_col, nc, rows)), out_s...]
    dot_general x5 -> x0, matrix products: 16.7 us -> none  [the longest x1 7.15 us: body(): cross_local = jnp.dot(panel_cols.T, matrix, precision=highest)]
    all_to_all x0 -> x1, waiting for transfers between devices: none -> 15.5 us  [body(): seen = lax.all_to_all(sent, ('row', 'col'), 0, 0)]
  transfers between devices with their start and end apart: 2 -> 1, of which waited for: 2 -> 1; matrix products, arithmetic and copies ran while one was open for 0% -> 0% of each run, Pallas kernels for 0% -> 0%
where the time goes in v1:
time: 47.4 us; the launch traced here: 47.1 us
  Pallas kernels  22 us (46%)
  waiting for transfers between devices  15.5 us (33%)
  starting transfers between devices  7.3 us (15%)
  local copies, waits for them, and re-layouts  1.57 us (3%)
  between operations  0.64 us (1%)
    pallas_call x1, Pallas kernels, body(): pl.pallas_call(functools.partial(kernel, (n_row, n_col, nc, rows)), out_s...  22 us
    all_to_all x1, waiting for transfers between devices, body(): seen = lax.all_to_all(sent, ('row', 'col'), 0, 0)  15.5 us
    all_to_all x1, starting transfers between devices, body(): seen = lax.all_to_all(sent, ('row', 'col'), 0, 0)  7.3 us
    broadcast_in_dim x1, local copies, waits for them, and re-layouts, body(): sent = jnp.broadcast_to(traces[None], (n_row * n_col, nc, rows))  1.57 us
  transfers between devices with their start and end apart: 1, of which 1 were waited for; matrix products, arithmetic and copies ran while one was open for 0% of the time, Pallas kernels for 0%

profile of v1, /device:TPU:0, one launch (start us, length us, event | category | flops | bytes accessed | tf_op | source)
XLA Modules:
  0.0 47.1 jit_solution(7000776000335942128)
XLA Ops:
  0.6 1.6 %broadcast_in_dim.2 = f32[32,8,512]{2,1,0:T(8,128)} broadcast(f32[8,512]{1,0:T(8,128)} %param.1), dimensions={1,2} | broadcast | bytes 540672 | tf_op jit(solution)/shard_map/broadcast_in_dim | solution.py:227
  2.2 7.3 %all-to-all-start = ((f32[32,8,512]{2,1,0:T(8,128)}), f32[32,8,512]{2,1,0:T(8,128)S(1)}, u32[]{:S(2)}, u32[]{:S(2)}) async-start(f32[32,8,512]{2,1,0:T(8,128)} %broadcast_in_dim.2), calls=%async_computation | async-start | bytes 1048576 | tf_op jit(solution)/shard_map/all_to_all | solution.py:228
  9.5 0.1 pad_add_fusion.place
  9.6 15.5 %all-to-all-done.seen = f32[32,8,512]{2,1,0:T(8,128)S(1)} async-done(((f32[32,8,512]{2,1,0:T(8,128)}), f32[32,8,512]{2,1,0:T(8,128)S(1)}, u32[]{:S(2)}, u32[]{:S(2)}) %all-to-all-start) | async-done | bytes 524320 | tf_op jit(solution)/shard_map/all_to_all | solution.py:228
  25.1 22.0 %shard_map.30 = (f32[512,2048]{1,0:T(8,128)}, f32[256,2048]{1,0:T(8,128)}) custom-call(s32[2]{0:T(128)S(1)} %pad_add_fusion.place, f32[32,8,512]{2,1,0:T(8,128)S(1)} %all-to-all-done.seen), custom_call_target="tpu_custom_call" | custom-call | tf_op jit(solution)/shard_map/pallas_call | solution.py:232
Async XLA Ops:
  2.2 22.9 %all-to-all-start = ((f32[32,8,512]{2,1,0:T(8,128)}), f32[32,8,512]{2,1,0:T(8,128)S(1)}, u32[]{:S(2)}, u32[]{:S(2)}) async-start(f32[32,8,512]{2,1,0:T(8,128)} %broadcast_in_dim.2), calls=%async_computation | async-start | bytes 1048576 | tf_op jit(solution)/shard_map/all_to_all | solution.py:228

commit v2 on v1

v2 whole, which is shorter than its diff:
```python
import functools

import jax
import jax.numpy as jnp
from jax import lax
from jax.experimental import pallas as pl
from jax.experimental.pallas import tpu as pltpu
from jax.sharding import PartitionSpec as P

TAPS = 256
WIDE = 256
LANES = 128
PANEL = 32
F32 = jnp.float32
BF16 = jnp.bfloat16
LEFT = (0, 0, 1, 0, 2, 1)
RIGHT = (0, 1, 0, 2, 0, 1)
SHORT = 3
NT = (((1,), (1,)), ((), ()))
TN = (((0,), (0,)), ((), ()))


def split(x, count=3):
    pieces = []
    for _ in range(count - 1):
        pieces.append(x.astype(BF16))
        x = x - pieces[-1].astype(F32)
    pieces.append(x.astype(BF16))
    return pieces


def dot(a, b, dims=None):
    if dims is None:
        return jnp.dot(a, b, preferred_element_type=F32)
    return lax.dot_general(a, b, dims, preferred_element_type=F32)


def joined(pieces, order, axis):
    return jnp.concatenate([pieces[i] for i in order], axis)


def row_of(x, j):
    return jnp.broadcast_to(x[j : j + 1, :], x.shape)


def inverse_factor(m, n):
    sub = lax.broadcasted_iota(jnp.int32, (8, LANES), 0)
    groups = PANEL // 8
    half = n // LANES
    for r0 in range(0, n, PANEL):
        cols = list(range(r0 // LANES, half)) + [half + i for i in range((r0 + PANEL - 1) // LANES + 1)]
        v = [{c: m[r0 + 8 * g : r0 + 8 * g + 8, LANES * c : LANES * (c + 1)] for c in cols} for g in range(groups)]
        for p in range(groups):
            tile, lane = divmod(r0 + 8 * p, LANES)
            col = [
                [jnp.broadcast_to(v[g][tile][:, lane + k : lane + k + 1], (8, LANES)) if g >= p else None for g in range(groups)]
                for k in range(8)
            ]
            pivots = jnp.ones((8, LANES), F32)
            for j in range(8):
                pivot = row_of(col[j][p], j)
                pivots = jnp.where(sub == j, pivot, pivots)
                if j == 7 and p == groups - 1:
                    continue
                inv = 1.0 / pivot
                first = p if j < 7 else p + 1
                factor = {g: col[j][g] * inv for g in range(first, groups)}
                if first == p:
                    factor[p] = jnp.where(sub > j, factor[p], 0.0)
                for k in range(j + 1, 8):
                    row = row_of(col[k][p], j)
                    for g in range(first, groups):
                        col[k][g] = col[k][g] - factor[g] * row
                for c in cols:
                    row = row_of(v[p][c], j)
                    for g in range(first, groups):
                        v[g][c] = v[g][c] - factor[g] * row
            scale = lax.rsqrt(pivots)
            for c in cols:
                v[p][c] = v[p][c] * scale
        for g in range(groups):
            for c in cols:
                m[r0 + 8 * g : r0 + 8 * g + 8, LANES * c : LANES * (c + 1)] = v[g][c]
        done = r0 + PANEL
        if done < n:
            pieces = {c: split(jnp.concatenate([v[g][c] for g in range(groups)], 0)) for c in cols}
            for a in range(done // LANES, half):
                left = jnp.concatenate([pieces[a][i] for i in LEFT], 0)
                skip = max(0, done - LANES * a)
                for c in cols:
                    if c >= a:
                        right = jnp.concatenate([pieces[c][i] for i in RIGHT], 0)
                        update = dot(left, right, TN)
                        m[LANES * a + skip : LANES * (a + 1), LANES * c : LANES * (c + 1)] -= update[skip:, :]


def strips(base, first):
    width = base.shape[1]
    strip = pltpu.roll(jnp.broadcast_to(base, (8, width)), first, 1, stride=1, stride_axis=0)
    return [pltpu.roll(strip, 8 * g, 1) if g else strip for g in range(LANES // 8)]


def tile_of(turned, block, lane):
    tiles = turned.shape[1] // LANES
    t = (lane - block) % tiles
    return turned[:, LANES * t : LANES * (t + 1)]


def expand(base, first, rows, ref, row, lane):
    for g, turned in enumerate(strips(base, first)):
        for h in range(rows // LANES):
            for j in range(TAPS // LANES):
                at = row + LANES * h + 8 * g
                ref[at : at + 8, lane + LANES * j : lane + LANES * (j + 1)] = tile_of(turned, h, j)


def expand_split(base, first, rows, refs, row, lane):
    turned = strips(base, first)
    for g in range(0, LANES // 8, 2):
        for h in range(rows // LANES):
            for j in range(TAPS // LANES):
                tile = jnp.concatenate([tile_of(turned[g], h, j), tile_of(turned[g + 1], h, j)], 0)
                at = row + LANES * h + 8 * g
                for ref, piece in zip(refs, split(tile, len(refs))):
                    ref[at : at + 16, lane + LANES * j : lane + LANES * (j + 1)] = piece


def turn_matrix():
    a = lax.broadcasted_iota(jnp.int32, (LANES, LANES), 0)
    b = lax.broadcasted_iota(jnp.int32, (LANES, LANES), 1)
    return (a + b == LANES - 1).astype(F32).astype(BF16)


def flip(x, turn):
    h, m, l = split(x)
    return dot(h, turn) + (dot(m, turn) + dot(l, turn))


def in_row(x, rows):
    return jnp.concatenate([x[r : r + 1, :] for r in rows], 1)


def read_lead(lead, first, n_row, n_col, per):
    blocks = n_row * per
    for r in range(n_row):
        for q in range(per):
            t = r * per + q
            lead[8 + t : 9 + t, :] = first[r * n_col, 0:1, LANES * q : LANES * (q + 1)]
    lead[0:8, :] = jnp.zeros((8, LANES), F32)
    lead[8 + blocks : 16 + blocks, :] = jnp.zeros((8, LANES), F32)


def shifted(lead, blocks, lowest, order):
    tail = TAPS // LANES
    step = lax.broadcasted_iota(jnp.int32, (blocks, LANES), 0)
    moved = []
    for a in range(lowest, tail + 1):
        keep = step < blocks - tail if a >= 0 else step + a < blocks - tail
        moved.append(jnp.where(keep, lead[8 + a : 8 + a + blocks, :], 0.0))
    return joined(split(jnp.concatenate(moved, 1)), order, 0)


def block_products(x, right, turn, order):
    left = dot(turn, joined(split(x), order, 0), NT).astype(BF16)
    return dot(left, right)


def skewed_sum(parts):
    size = 8
    while len(parts) > 1:
        parts = [parts[i] + pltpu.roll(parts[i + 1], size, 1) for i in range(0, len(parts), 2)]
        size *= 2
    rows = [pltpu.roll(parts[0][r : r + 8, :], 0, 1, stride=1, stride_axis=0) for r in range(0, parts[0].shape[0], 8)]
    return [jnp.sum(x, axis=0, keepdims=True) for x in rows]


def factor_kernel(sizes, place, first, factor_high, factor_low, basis_high, basis_low, lead, gram, window):
    n_row, n_col, nc, rows = sizes
    per = rows // LANES
    blocks = n_row * per
    tail = TAPS // LANES
    scale = 1.0 / (n_row * rows)
    read_lead(lead, first, n_row, n_col, per)
    turn = turn_matrix()
    zeros = jnp.zeros((1, TAPS), F32)

    last = lead[8 + blocks - tail : 8 + blocks, :]
    expand(jnp.concatenate([in_row(last, range(tail)), zeros], 1), 0, TAPS, window, 0, 0)
    left = joined(split(window[0:TAPS, :]), LEFT, 1)
    short_left = window[0:TAPS, :]
    expand(jnp.concatenate([in_row(flip(last, turn), reversed(range(tail))), zeros], 1), 1 + TAPS, TAPS, window, 0, 0)
    extra = dot(left, joined(split(window[0:TAPS, :]), RIGHT, 0))

    right = shifted(lead, blocks, -1, RIGHT)
    z = block_products(lead[8 : 8 + blocks, :], right, turn, LEFT)
    lags = skewed_sum([z[r : r + 8, :] for r in range(0, LANES, 8)])[0]
    expand(lags, 1 + TAPS, WIDE, gram, 0, 0)
    gram[:, 0:WIDE] = (gram[:, 0:WIDE] + extra) * scale
    a = lax.broadcasted_iota(jnp.int32, (WIDE, WIDE), 0)
    b = lax.broadcasted_iota(jnp.int32, (WIDE, WIDE), 1)
    gram[:, WIDE:] = (a == b).astype(F32)
    inverse_factor(gram, WIDE)

    inverse = gram[:, WIDE:]
    pieces = split(inverse, 2)
    scaled = split(inverse * scale, 2)
    fold = split(dot(joined(scaled, LEFT[:SHORT], 1), joined(split(short_left, 2), RIGHT[:SHORT], 0)), 2)
    for ref, a, b in ((factor_high, scaled[0], fold[0]), (factor_low, scaled[1], fold[1])):
        ref[:, 0:WIDE] = a
        ref[:, WIDE:] = b

    start = place[0] * per
    own = flip(lead[pl.ds(8 + start - tail, per + tail), :], turn)
    expand(in_row(own, reversed(range(per + tail))), 1 + TAPS, rows, window, 0, 0)
    basis = dot(joined(split(window[...], 2), LEFT[:SHORT], 1), joined(pieces, RIGHT[:SHORT], 1), NT)
    basis_high[...], basis_low[...] = split(basis, 2)


def update_kernel(
    sizes, place, first, seen, factor_high, factor_low, basis_high, basis_low, over_out, coup_out,
    natural, lead, products, right_high, right_low, over, coup, over_sems, coup_sems,
):
    n_row, n_col, nc, rows = sizes
    per = rows // LANES
    blocks = n_row * per
    tail = TAPS // LANES
    turn = turn_matrix()
    zeros = jnp.zeros((1, TAPS), F32)
    read_lead(lead, first, n_row, n_col, per)
    for r in range(n_row):
        for q in range(per):
            t = r * per + q
            natural[t * nc : (t + 1) * nc, :] = seen[r, :, LANES * q : LANES * (q + 1)]

    start = place[0] * per
    rows_of = lambda t: natural[pl.ds(pl.multiple_of(t * nc, nc), nc), :]
    history = jnp.where(place[0] > 0, 1.0, 0.0)
    near = [rows_of(jnp.maximum(start + q, 0)) * (history if q < 0 else 1.0) for q in range(-tail, per)]
    near += [rows_of(blocks - tail + q) for q in range(tail)]
    near = flip(jnp.concatenate(near, 0), turn)

    right = shifted(lead, blocks, -tail, (0, 1, 0, 1))
    left = [joined(split(natural[pl.ds(c, blocks, stride=nc), :], 2), (0, 0, 1, 1), 0) for c in range(nc)]
    left = dot(turn, jnp.concatenate(left, 0), NT).astype(BF16)
    for c in range(nc):
        products[c] = dot(left[:, 4 * blocks * c : 4 * blocks * (c + 1)], right)
    parts = [products[:, r : r + 8, :].reshape(nc * 8, products.shape[2]) for r in range(0, LANES, 8)]
    lags = skewed_sum(parts)
    for c in range(nc):
        expand_split(lags[c], 1 + TAPS, TAPS, (right_high.at[c], right_low.at[c]), 0, 0)
        last = [(per + tail + q) * nc + c for q in reversed(range(tail))]
        expand_split(
            jnp.concatenate([in_row(near, last), zeros], 1), 1 + TAPS, TAPS, (right_high.at[c], right_low.at[c]), TAPS, 0
        )
    factor = jnp.concatenate([factor_high[...], factor_high[...], factor_low[...]], 1)
    basis = jnp.concatenate([basis_high[...], basis_high[...], basis_low[...]], 1)
    copies = []

    def couple(c):
        at = slice(c * TAPS, (c + 1) * TAPS)
        coupling = dot(factor, joined((right_high[c], right_low[c]), RIGHT[:SHORT], 0))
        coup[:, at] = coupling
        copies.append(pltpu.make_async_copy(coup.at[:, at], coup_out.at[:, at], coup_sems.at[c]))
        copies[-1].start()
        expand(in_row(near, [q * nc + c for q in reversed(range(per + tail))]), 1 + TAPS, rows, over, 0, c * TAPS)
        return joined(split(coupling, 2), RIGHT[:SHORT], 0)

    ahead = couple(0)
    for c in range(nc):
        at = slice(c * TAPS, (c + 1) * TAPS)
        now = ahead
        if c + 1 < nc:
            ahead = couple(c + 1)
        rest = over[:, at] - dot(basis, now)
        if c * TAPS < WIDE:
            rest = jnp.where(place[1] == 0, basis_high[...].astype(F32) + basis_low[...].astype(F32), rest)
        over[:, at] = rest
        copies.append(pltpu.make_async_copy(over.at[:, at], over_out.at[:, at], over_sems.at[c]))
        copies[-1].start()
    for copy in copies:
        copy.wait()


def factor_call(sizes, place, first):
    n_row, n_col, nc, rows = sizes
    blocks = n_row * rows // LANES
    small = jax.ShapeDtypeStruct((WIDE, WIDE + TAPS), BF16)
    tall = jax.ShapeDtypeStruct((rows, WIDE), BF16)
    return pl.pallas_call(
        functools.partial(factor_kernel, sizes),
        out_shape=(small, small, tall, tall),
        in_specs=[pl.BlockSpec(memory_space=pltpu.SMEM), pl.BlockSpec(memory_space=pltpu.VMEM)],
        out_specs=[pl.BlockSpec(memory_space=pltpu.VMEM)] * 4,
        scratch_shapes=[
            pltpu.VMEM((blocks + 16, LANES), F32),
            pltpu.VMEM((WIDE, 2 * WIDE), F32),
            pltpu.VMEM((max(rows, TAPS), TAPS), F32),
        ],
        compiler_params=pltpu.CompilerParams(vmem_limit_bytes=16 * 2**20),
        cost_estimate=pl.CostEstimate(flops=10**10, bytes_accessed=10**6, transcendentals=0),
    )(place, first)


def update_call(sizes, place, first, seen, parts):
    n_row, n_col, nc, rows = sizes
    blocks = n_row * rows // LANES
    return pl.pallas_call(
        functools.partial(update_kernel, sizes),
        out_shape=(
            jax.ShapeDtypeStruct((rows, nc * TAPS), F32),
            jax.ShapeDtypeStruct((WIDE, nc * TAPS), F32),
        ),
        in_specs=[pl.BlockSpec(memory_space=pltpu.SMEM)] + [pl.BlockSpec(memory_space=pltpu.VMEM)] * 6,
        out_specs=[pl.BlockSpec(memory_space=pl.ANY)] * 2,
        scratch_shapes=[
            pltpu.VMEM((blocks * nc, LANES), F32),
            pltpu.VMEM((blocks + 16, LANES), F32),
            pltpu.VMEM((nc, LANES, 2 * TAPS + LANES), F32),
            pltpu.VMEM((nc, 2 * TAPS, TAPS), BF16),
            pltpu.VMEM((nc, 2 * TAPS, TAPS), BF16),
            pltpu.VMEM((rows, nc * TAPS), F32),
            pltpu.VMEM((WIDE, nc * TAPS), F32),
            pltpu.SemaphoreType.DMA((nc,)),
            pltpu.SemaphoreType.DMA((nc,)),
        ],
        compiler_params=pltpu.CompilerParams(vmem_limit_bytes=40 * 2**20),
        cost_estimate=pl.CostEstimate(flops=10**10, bytes_accessed=10**7, transcendentals=0),
    )(place, first, seen, *parts)


def body(traces):
    n_row, n_col = lax.axis_size("row"), lax.axis_size("col")
    nc, rows = traces.shape
    sizes = (n_row, n_col, nc, rows)
    first = lax.all_to_all(jnp.broadcast_to(traces[None, 0:1], (n_row * n_col, 1, rows)), ("row", "col"), 0, 0)
    seen = lax.all_to_all(jnp.broadcast_to(traces[None], (n_row, nc, rows)), "row", 0, 0)
    place = jnp.stack([lax.axis_index("row"), lax.axis_index("col")]).astype(jnp.int32)
    parts = factor_call(sizes, place, first)
    return update_call(sizes, place, first, seen, parts)


def solution(mesh):
    return jax.shard_map(
        body,
        mesh=mesh,
        in_specs=(P("col", "row"),),
        out_specs=(P("row", "col"), P(None, "col")),
        check_vma=False,
    )
```

time: 47.4 us -> 41.3 us (0.87)
  waiting for transfers between devices: 15.5 us -> 8.02 us
  Pallas kernels: 22 us -> 18.4 us
  starting transfers between devices: 7.3 us -> 10.8 us
  local copies, waits for them, and re-layouts: 1.57 us -> 2.83 us
    all_to_all x1 -> x2, waiting for transfers between devices: 15.5 us -> 8.02 us  [the longest x1 7.33 us: body(): lax.all_to_all(jnp.broadcast_to(traces[None, 0:1], (n_row * n_col, 1, row...]
    pallas_call x1 -> x2, Pallas kernels: 22 us -> 18.4 us  [the longest x1 9.67 us: factor_call(): pl.pallas_call(functools.partial(factor_kernel, sizes), out_shape=(small,...]
    all_to_all x1 -> x2, starting transfers between devices: 7.3 us -> 10.8 us  [the longest x1 7.3 us: body(): lax.all_to_all(jnp.broadcast_to(traces[None, 0:1], (n_row * n_col, 1, row...]
    slice x0 -> x1, local copies, waits for them, and re-layouts: none -> 0.72 us  [body(): traces[None, 0:1]]
    broadcast_in_dim x1 -> x2, local copies, waits for them, and re-layouts: 1.57 us -> 2.11 us  [the longest x1 1.44 us: body(): jnp.broadcast_to(traces[None], (n_row, nc, rows))]
  transfers between devices with their start and end apart: 1 -> 2, of which waited for: 1 -> 2; matrix products, arithmetic and copies ran while one was open for 0% -> 0% of each run, Pallas kernels for 0% -> 24%
where the time goes in v2:
time: 41.3 us; the launch traced here: 40.8 us
  Pallas kernels  18.4 us (45%)
  starting transfers between devices  10.8 us (26%)
  waiting for transfers between devices  8.02 us (19%)
  local copies, waits for them, and re-layouts  2.83 us (7%)
  between operations  0.66 us (2%)
    pallas_call x1, Pallas kernels, factor_call(): pl.pallas_call(functools.partial(factor_kernel, sizes), out_shape=(small,...  9.67 us
    pallas_call x1, Pallas kernels, update_call(): pl.pallas_call(functools.partial(update_kernel, sizes), out_shape=(jax.Sh...  8.73 us
    all_to_all x1, waiting for transfers between devices, body(): lax.all_to_all(jnp.broadcast_to(traces[None, 0:1], (n_row * n_col, 1, row...  7.33 us
    all_to_all x1, starting transfers between devices, body(): lax.all_to_all(jnp.broadcast_to(traces[None, 0:1], (n_row * n_col, 1, row...  7.3 us
    all_to_all x1, starting transfers between devices, body(): lax.all_to_all(jnp.broadcast_to(traces[None], (n_row, nc, rows)), 'row',...  3.53 us
    broadcast_in_dim x1, local copies, waits for them, and re-layouts, body(): jnp.broadcast_to(traces[None], (n_row, nc, rows))  1.44 us
  transfers between devices with their start and end apart: 2, of which 2 were waited for; matrix products, arithmetic and copies ran while one was open for 0% of the time, Pallas kernels for 24%

profile of v2, /device:TPU:0, one launch (start us, length us, event | category | flops | bytes accessed | tf_op | source)
XLA Modules:
  0.0 40.8 jit_solution(1245190359711621108)
XLA Ops:
  0.6 0.7 %slice.3 = f32[1,512]{1,0:T(1,128)S(1)} slice(f32[8,512]{1,0:T(8,128)} %param.1), slice={[0:1], [0:512]} | slice | bytes 4096 | tf_op jit(solution)/shard_map/slice | solution.py:335
  1.4 0.7 %broadcast_in_dim.7 = f32[32,1,512]{2,1,0:T(1,128)} broadcast(f32[512]{0:T(512)S(1)} %bitcast.3), dimensions={2} | broadcast | bytes 67584 | tf_op jit(solution)/shard_map/broadcast_in_dim | solution.py:335
  2.0 7.3 %all-to-all-start = ((f32[32,1,512]{2,1,0:T(1,128)}), f32[32,1,512]{2,1,0:T(1,128)S(1)}, u32[]{:S(2)}, u32[]{:S(2)}) async-start(f32[32,1,512]{2,1,0:T(1,128)} %broadcast_in_dim.7), calls=%async_computation | async-start | bytes 131072 | tf_op jit(solution)/shard_map/all_to_all | solution.py:335
  9.3 0.1 pad_add_fusion.place
  9.4 7.3 %all-to-all-done.first = f32[32,1,512]{2,1,0:T(1,128)S(1)} async-done(((f32[32,1,512]{2,1,0:T(1,128)}), f32[32,1,512]{2,1,0:T(1,128)S(1)}, u32[]{:S(2)}, u32[]{:S(2)}) %all-to-all-start) | async-done | bytes 65568 | tf_op jit(solution)/shard_map/all_to_all | solution.py:335
  16.7 1.4 %broadcast_in_dim.16 = f32[16,8,512]{2,1,0:T(8,128)} broadcast(f32[8,512]{1,0:T(8,128)} %param.1), dimensions={1,2} | broadcast | bytes 278528 | tf_op jit(solution)/shard_map/broadcast_in_dim | solution.py:336
  18.2 3.5 %all-to-all-start.1 = ((f32[16,8,512]{2,1,0:T(8,128)}), f32[16,8,512]{2,1,0:T(8,128)S(1)}, u32[]{:S(2)}, u32[]{:S(2)}) async-start(f32[16,8,512]{2,1,0:T(8,128)} %broadcast_in_dim.16), calls=%async_computation.1 | async-start | bytes 524288 | tf_op jit(solution)/shard_map/all_to_all | solution.py:336
  21.7 9.7 %shard_map.30 = (bf16[256,512]{1,0:T(8,128)(2,1)S(1)}, bf16[256,512]{1,0:T(8,128)(2,1)S(1)}, bf16[512,256]{1,0:T(8,128)(2,1)S(1)}, bf16[512,256]{1,0:T(8,128)(2,1)S(1)}) custom-call(s32[2]{0:T(128)S(1)} %pad_add_fusion.place, f32[32,1,512]{2,1,0:T(1,128)S(1)} %all-to-all-done.first), custom_call_target="tpu_custom_call" | custom-call | flops 10000000000 | bytes 1000000 | tf_op jit(solution)/shard_map/pallas_call | solution.py:289
  31.4 0.7 %all-to-all-done.1.seen = f32[16,8,512]{2,1,0:T(8,128)S(1)} async-done(((f32[16,8,512]{2,1,0:T(8,128)}), f32[16,8,512]{2,1,0:T(8,128)S(1)}, u32[]{:S(2)}, u32[]{:S(2)}) %all-to-all-start.1) | async-done | bytes 262176 | tf_op jit(solution)/shard_map/all_to_all | solution.py:336
  32.1 8.7 %shard_map.31 = (f32[512,2048]{1,0:T(8,128)}, f32[256,2048]{1,0:T(8,128)}) custom-call(s32[2]{0:T(128)S(1)} %pad_add_fusion.place, f32[32,1,512]{2,1,0:T(1,128)S(1)} %all-to-all-done.first, f32[16,8,512]{2,1,0:T(8,128)S(1)} %all-to-all-done.1.seen, bf16[256,512]{1,0:T(8,128)(2,1)S(1)} %get-tuple-element.6.factor_high, ...), custom_call_target="tpu_custom_call" | custom-call | flops 10000000000 | bytes 10000000 | tf_op jit(solution)/shard_map/pallas_call | solution.py:307
Async XLA Ops:
  2.0 14.7 %all-to-all-start = ((f32[32,1,512]{2,1,0:T(1,128)}), f32[32,1,512]{2,1,0:T(1,128)S(1)}, u32[]{:S(2)}, u32[]{:S(2)}) async-start(f32[32,1,512]{2,1,0:T(1,128)} %broadcast_in_dim.7), calls=%async_computation | async-start | bytes 131072 | tf_op jit(solution)/shard_map/all_to_all | solution.py:335
  18.2 13.9 %all-to-all-start.1 = ((f32[16,8,512]{2,1,0:T(8,128)}), f32[16,8,512]{2,1,0:T(8,128)S(1)}, u32[]{:S(2)}, u32[]{:S(2)}) async-start(f32[16,8,512]{2,1,0:T(8,128)} %broadcast_in_dim.16), calls=%async_computation.1 | async-start | bytes 524288 | tf_op jit(solution)/shard_map/all_to_all | solution.py:336

commit v3 on v2

v3 whole, which is shorter than its diff:
```python
import functools

import jax
import jax.numpy as jnp
from jax import lax
from jax.experimental import pallas as pl
from jax.experimental.pallas import tpu as pltpu
from jax.sharding import PartitionSpec as P

TAPS = 256
WIDE = 256
LANES = 128
PANEL = 32
SPAN = 16
FIRST = True
F32 = jnp.float32
BF16 = jnp.bfloat16
LEFT = (0, 0, 1, 0, 2, 1)
RIGHT = (0, 1, 0, 2, 0, 1)
SHORT = 3
NT = (((1,), (1,)), ((), ()))
TN = (((0,), (0,)), ((), ()))


def split(x, count=3):
    pieces = []
    for _ in range(count - 1):
        pieces.append(x.astype(BF16))
        x = x - pieces[-1].astype(F32)
    pieces.append(x.astype(BF16))
    return pieces


def dot(a, b, dims=None):
    if dims is None:
        return jnp.dot(a, b, preferred_element_type=F32)
    return lax.dot_general(a, b, dims, preferred_element_type=F32)


def joined(pieces, order, axis):
    return jnp.concatenate([pieces[i] for i in order], axis)


def row_of(x, j):
    return jnp.broadcast_to(x[j : j + 1, :], x.shape)


def inverse_factor(m, n, pause):
    sub = lax.broadcasted_iota(jnp.int32, (8, LANES), 0)
    odd = sub % 2 == 1
    groups = PANEL // 8
    half = n // LANES
    for r0 in range(0, n, PANEL):
        tiles = list(range(r0 // LANES, half)) + [half + i for i in range((r0 + PANEL - 1) // LANES + 1)]
        v = [{c: m[r0 + 8 * g : r0 + 8 * g + 8, LANES * c : LANES * (c + 1)] for c in tiles} for g in range(groups)]
        pivots = [None] * groups
        for s in range(0, groups, SPAN // 8):
            col = [[None] * groups for _ in range(SPAN)]
            for k in range(SPAN):
                tile, lane = divmod(r0 + 8 * s + k, LANES)
                for g in range(s + k // 8, groups):
                    col[k][g] = jnp.broadcast_to(v[g][tile][:, lane : lane + 1], (8, LANES))
            for j in range(0, SPAN, 2):
                p, i = s + j // 8, j % 8
                x, y = col[j], col[j + 1]
                pivot = [row_of(x[p], i), row_of(x[p], i + 1), row_of(y[p], i + 1)]
                pivots[p] = pivot if i == 0 else [jnp.where(sub < i, old, new) for old, new in zip(pivots[p], pivot)]
                first = p if i < 6 else p + 1
                if first == groups:
                    continue
                a, b, c = pivot
                inv = 1.0 / (a * c - b * b)
                a, b, c = a * inv, b * inv, c * inv
                fx, fy = {}, {}
                for g in range(first, groups):
                    fx[g] = x[g] * c - y[g] * b
                    fy[g] = y[g] * a - x[g] * b
                    if g == p:
                        fx[g] = jnp.where(sub > i + 1, fx[g], 0.0)
                        fy[g] = jnp.where(sub > i + 1, fy[g], 0.0)
                for k in range(j + 2, SPAN):
                    gk = s + k // 8
                    rx, ry = row_of(x[gk], k % 8), row_of(y[gk], k % 8)
                    for g in range(gk, groups):
                        col[k][g] = col[k][g] - (fx[g] * rx + fy[g] * ry)
                for t in tiles:
                    rx, ry = row_of(v[p][t], i), row_of(v[p][t], i + 1)
                    for g in range(first, groups):
                        v[g][t] = v[g][t] - (fx[g] * rx + fy[g] * ry)
        for g in range(groups):
            a, b, c = pivots[g]
            ratio = b / a
            scale = lax.rsqrt(jnp.where(odd, c - b * ratio, a))
            ratio = jnp.where(odd, ratio, 0.0)
            for t in tiles:
                v[g][t] = (v[g][t] - ratio * pltpu.roll(v[g][t], 1, 0)) * scale
                m[r0 + 8 * g : r0 + 8 * g + 8, LANES * t : LANES * (t + 1)] = v[g][t]
        done = r0 + PANEL
        if done < n:
            pieces = {c: split(jnp.concatenate([v[g][c] for g in range(groups)], 0)) for c in tiles}
            right = {c: joined(pieces[c], RIGHT, 0) for c in tiles}
            updates = []
            for a in range(done // LANES, half):
                left = joined(pieces[a], LEFT, 0)
                updates += [(a, c, dot(left, right[c], TN)) for c in tiles if c >= a]
            pause()
            for a, c, update in updates:
                skip = max(0, done - LANES * a)
                m[LANES * a + skip : LANES * (a + 1), LANES * c : LANES * (c + 1)] -= update[skip:, :]


def shifted_rows(base, first, rows, step):
    strip = pltpu.roll(jnp.broadcast_to(base, (rows, base.shape[1])), first, 1, stride=1, stride_axis=0)
    return [strip[r : r + step, :] for r in range(0, rows, step)]


def tile_of(turned, block, lane):
    tiles = turned.shape[1] // LANES
    t = (lane - block) % tiles
    return turned[:, LANES * t : LANES * (t + 1)]


def expand(base, first, rows, ref, row, lane):
    for g, turned in enumerate(shifted_rows(base, first, LANES, 8)):
        for h in range(rows // LANES):
            for j in range(TAPS // LANES):
                at = row + LANES * h + 8 * g
                ref[at : at + 8, lane + LANES * j : lane + LANES * (j + 1)] = tile_of(turned, h, j)


def expand_split(base, first, rows, refs):
    (strip,) = shifted_rows(base, first, 16, 16)
    for ref, piece in zip(refs, split(strip, len(refs))):
        for g in range(0, LANES // 16):
            turned = pltpu.roll(piece, 16 * g, 1) if g else piece
            for h in range(rows // LANES):
                for j in range(TAPS // LANES):
                    at = LANES * h + 16 * g
                    ref[at : at + 16, LANES * j : LANES * (j + 1)] = tile_of(turned, h, j)


def run(steps):
    for _ in steps:
        pass


def turn_matrix():
    a = lax.broadcasted_iota(jnp.int32, (LANES, LANES), 0)
    b = lax.broadcasted_iota(jnp.int32, (LANES, LANES), 1)
    return (a + b == LANES - 1).astype(F32).astype(BF16)


def flip(x, turn):
    h, m, l = split(x)
    return dot(h, turn) + (dot(m, turn) + dot(l, turn))


def in_row(x, rows):
    return jnp.concatenate([x[r : r + 1, :] for r in rows], 1)


def read_lead(lead, seen, other, my_col, n_row, per):
    blocks = n_row * per
    here = my_col == 0
    for r in range(n_row):
        for q in range(per):
            t = r * per + q
            at = slice(LANES * q, LANES * (q + 1))
            lead[8 + t : 9 + t, :] = jnp.where(here, seen[r, 0:1, at], other[r, 0:1, at])
    lead[0:8, :] = jnp.zeros((8, LANES), F32)
    lead[8 + blocks : 16 + blocks, :] = jnp.zeros((8, LANES), F32)


def shifted(lead, blocks, lowest, order):
    tail = TAPS // LANES
    step = lax.broadcasted_iota(jnp.int32, (blocks, LANES), 0)
    moved = []
    for a in range(lowest, tail + 1):
        keep = step < blocks - tail if a >= 0 else step + a < blocks - tail
        moved.append(jnp.where(keep, lead[8 + a : 8 + a + blocks, :], 0.0))
    return joined(split(jnp.concatenate(moved, 1)), order, 0)


def block_products(x, right, turn, order):
    left = dot(turn, joined(split(x), order, 0), NT).astype(BF16)
    return dot(left, right)


def skewed_sum(z):
    return jnp.sum(pltpu.roll(z, 0, 1, stride=1, stride_axis=0), axis=0, keepdims=True)


def kernel(
    sizes, other, seen, over_out, coup_out,
    natural, lead, gram, window, products, low_high, low_low, cross, cross_high, cross_low, over, coup, over_sems, coup_sems,
):
    n_row, n_col, nc, rows = sizes
    per = rows // LANES
    blocks = n_row * per
    tail = TAPS // LANES
    scale = 1.0 / (n_row * rows)
    my_row, my_col = lax.axis_index("row"), lax.axis_index("col")
    start = my_row * per
    turn = turn_matrix()
    zeros = jnp.zeros((1, TAPS), F32)
    read_lead(lead, seen, other, my_col, n_row, per)

    z = block_products(lead[8 : 8 + blocks, :], shifted(lead, blocks, -1, RIGHT), turn, LEFT)
    lags = skewed_sum(z)

    last = lead[8 + blocks - tail : 8 + blocks, :]
    expand(jnp.concatenate([in_row(last, range(tail)), zeros], 1), 0, TAPS, window, 0, 0)
    left = split(window[0:TAPS, :])
    tail_left = joined(left, LEFT[:SHORT], 1)
    expand(jnp.concatenate([in_row(flip(last, turn), reversed(range(tail))), zeros], 1), 1 + TAPS, TAPS, gram, 0, WIDE)
    extra = dot(joined(left, LEFT, 1), joined(split(gram[:, WIDE:]), RIGHT, 0))

    expand(lags, 1 + TAPS, WIDE, gram, 0, 0)
    gram[:, 0:WIDE] = (gram[:, 0:WIDE] + extra) * scale
    a = lax.broadcasted_iota(jnp.int32, (WIDE, WIDE), 0)
    b = lax.broadcasted_iota(jnp.int32, (WIDE, WIDE), 1)
    gram[:, WIDE:] = (a == b).astype(F32)

    for r in range(n_row):
        for q in range(per):
            t = r * per + q
            natural[t * nc : (t + 1) * nc, :] = seen[r, :, LANES * q : LANES * (q + 1)]
    rows_of = lambda t: natural[pl.ds(pl.multiple_of(t * nc, nc), nc), :]
    history = jnp.where(my_row > 0, 1.0, 0.0)
    near = [rows_of(jnp.maximum(start + q, 0)) * (history if q < 0 else 1.0) for q in range(-tail, per)]
    near += [rows_of(blocks - tail + q) for q in range(tail)]
    near = flip(jnp.concatenate(near, 0), turn)
    own = flip(lead[pl.ds(8 + start - tail, per + tail), :], turn)
    expand(in_row(own, reversed(range(per + tail))), 1 + TAPS, rows, window, 0, 0)
    own_rows = joined(split(window[0:rows, :], 2), LEFT[:SHORT], 1)
    right = shifted(lead, blocks, -tail, (0, 1, 0, 1))
    left = [joined(split(natural[pl.ds(c, blocks, stride=nc), :], 2), (0, 0, 1, 1), 0) for c in range(nc)]
    left = dot(turn, jnp.concatenate(left, 0), NT).astype(BF16)

    def steps():
        for c in range(nc):
            products[c] = dot(left[:, 4 * blocks * c : 4 * blocks * (c + 1)], right)
        for c in range(nc):
            last = [(per + tail + q) * nc + c for q in reversed(range(tail))]
            refs = (low_high.at[c], low_low.at[c])
            expand_split(jnp.concatenate([in_row(near, last), zeros], 1), 1 + TAPS, TAPS, refs)
        yield
        for c in range(nc):
            expand(skewed_sum(products[c]), 1 + TAPS, TAPS, cross, 0, c * TAPS)
            if c % 2 == 1:
                yield
        for c in range(nc):
            at = slice(c * TAPS, (c + 1) * TAPS)
            whole = cross[:, at] + dot(tail_left, joined((low_high[c], low_low[c]), RIGHT[:SHORT], 0))
            cross_high[c], cross_low[c] = split(whole * scale, 2)
            if c % 4 == 3:
                yield

    rest = steps()
    if FIRST:
        run(rest)
    inverse_factor(gram, WIDE, lambda: next(rest, None))
    run(rest)

    pieces = split(gram[:, WIDE:], 2)
    factor = joined(pieces, LEFT[:SHORT], 1)
    panel = dot(own_rows, joined(pieces, RIGHT[:SHORT], 1), NT)
    basis = joined(split(panel, 2), LEFT[:SHORT], 1)
    copies = []

    def couple(c):
        at = slice(c * TAPS, (c + 1) * TAPS)
        coupling = dot(factor, joined((cross_high[c], cross_low[c]), RIGHT[:SHORT], 0))
        coup[:, at] = coupling
        copies.append(pltpu.make_async_copy(coup.at[:, at], coup_out.at[:, at], coup_sems.at[c]))
        copies[-1].start()
        expand(in_row(near, [q * nc + c for q in reversed(range(per + tail))]), 1 + TAPS, rows, over, 0, c * TAPS)
        return joined(split(coupling, 2), RIGHT[:SHORT], 0)

    ahead = couple(0)
    for c in range(nc):
        at = slice(c * TAPS, (c + 1) * TAPS)
        now = ahead
        if c + 1 < nc:
            ahead = couple(c + 1)
        rest = over[:, at] - dot(basis, now)
        if c * TAPS < WIDE:
            rest = jnp.where(my_col == 0, panel, rest)
        over[:, at] = rest
        copies.append(pltpu.make_async_copy(over.at[:, at], over_out.at[:, at], over_sems.at[c]))
        copies[-1].start()
    for copy in copies:
        copy.wait()


def call(sizes, other, seen):
    n_row, n_col, nc, rows = sizes
    blocks = n_row * rows // LANES
    return pl.pallas_call(
        functools.partial(kernel, sizes),
        out_shape=(
            jax.ShapeDtypeStruct((rows, nc * TAPS), F32),
            jax.ShapeDtypeStruct((WIDE, nc * TAPS), F32),
        ),
        in_specs=[pl.BlockSpec(memory_space=pltpu.VMEM)] * 2,
        out_specs=[pl.BlockSpec(memory_space=pl.ANY)] * 2,
        scratch_shapes=[
            pltpu.VMEM((blocks * nc, LANES), F32),
            pltpu.VMEM((blocks + 16, LANES), F32),
            pltpu.VMEM((WIDE, 2 * WIDE), F32),
            pltpu.VMEM((max(rows, TAPS), TAPS), F32),
            pltpu.VMEM((nc, LANES, 2 * TAPS + LANES), F32),
            pltpu.VMEM((nc, TAPS, TAPS), BF16),
            pltpu.VMEM((nc, TAPS, TAPS), BF16),
            pltpu.VMEM((WIDE, nc * TAPS), F32),
            pltpu.VMEM((nc, TAPS, TAPS), BF16),
            pltpu.VMEM((nc, TAPS, TAPS), BF16),
            pltpu.VMEM((rows, nc * TAPS), F32),
            pltpu.VMEM((WIDE, nc * TAPS), F32),
            pltpu.SemaphoreType.DMA((nc,)),
            pltpu.SemaphoreType.DMA((nc,)),
        ],
        compiler_params=pltpu.CompilerParams(vmem_limit_bytes=24 * 2**20),
    )(other, seen)


def body(traces):
    n_row, n_col = lax.axis_size("row"), lax.axis_size("col")
    nc, rows = traces.shape
    seen = lax.all_to_all(jnp.broadcast_to(traces[None], (n_row, nc, rows)), "row", 0, 0)
    col = lax.axis_index("col")
    first, step = seen[:, 0:1], 1
    while step < n_col:
        other = lax.ppermute(first, "col", [(i, i + step) for i in range(min(step, n_col - step))])
        first, step = jnp.where(col < step, first, other), 2 * step
    return call((n_row, n_col, nc, rows), other, seen)


def solution(mesh):
    return jax.shard_map(
        body,
        mesh=mesh,
        in_specs=(P("col", "row"),),
        out_specs=(P("row", "col"), P(None, "col")),
        check_vma=False,
    )
```

time: 41.3 us -> 34.3 us (0.83)
  blocking collectives: 0 us -> 18 us
  starting transfers between devices: 10.8 us -> 1.29 us
  waiting for transfers between devices: 8.02 us -> 0.84 us
  Pallas kernels: 18.4 us -> 12.5 us
  local copies, waits for them, and re-layouts: 2.83 us -> 0.75 us
    all_to_all x0 -> x1, blocking collectives: none -> 18 us  [body(): lax.all_to_all(jnp.broadcast_to(traces[None], (n_row, nc, rows)), 'row',...]
    all_to_all x2 -> x0, starting transfers between devices: 10.8 us -> none  [the longest x1 7.3 us: body(): lax.all_to_all(jnp.broadcast_to(traces[None, 0:1], (n_row * n_col, 1, row...]
    all_to_all x2 -> x0, waiting for transfers between devices: 8.02 us -> none  [the longest x1 7.33 us: body(): lax.all_to_all(jnp.broadcast_to(traces[None, 0:1], (n_row * n_col, 1, row...]
    pallas_call x2 -> x1, Pallas kernels: 18.4 us -> 12.5 us  [call(): pl.pallas_call(functools.partial(kernel, sizes), out_shape=(jax.ShapeDtyp...]
    ppermute x0 -> x1, starting transfers between devices: none -> 1.29 us  [body(): lax.ppermute(first, 'col', [(i, i + step) for i in range(min(step, n_col...]
    ppermute x0 -> x1, waiting for transfers between devices: none -> 0.84 us  [body(): lax.ppermute(first, 'col', [(i, i + step) for i in range(min(step, n_col...]
    broadcast_in_dim x1, local copies, waits for them, and re-layouts: 1.44 us -> 0.74 us  [body(): jnp.broadcast_to(traces[None], (n_row, nc, rows))]
    slice x1, local copies, waits for them, and re-layouts: 0.72 us -> 0.02 us  [body(): first, step = (seen[:, 0:1], 1)]
  transfers between devices with their start and end apart: 2 -> 1, of which waited for: 2 -> 1; matrix products, arithmetic and copies ran while one was open for 0% -> 0% of each run, Pallas kernels for 24% -> 0%
where the time goes in v3:
time: 34.3 us; the launch traced here: 34 us
  blocking collectives  18 us (52%)
  Pallas kernels  12.5 us (36%)
  starting transfers between devices  1.29 us (4%)
  waiting for transfers between devices  0.84 us (2%)
  local copies, waits for them, and re-layouts  0.75 us (2%)
  between operations  0.65 us (2%)
    all_to_all x1, blocking collectives, body(): lax.all_to_all(jnp.broadcast_to(traces[None], (n_row, nc, rows)), 'row',...  18 us
    pallas_call x1, Pallas kernels, call(): pl.pallas_call(functools.partial(kernel, sizes), out_shape=(jax.ShapeDtyp...  12.5 us
    ppermute x1, starting transfers between devices, body(): lax.ppermute(first, 'col', [(i, i + step) for i in range(min(step, n_col...  1.29 us
    ppermute x1, waiting for transfers between devices, body(): lax.ppermute(first, 'col', [(i, i + step) for i in range(min(step, n_col...  0.84 us
    broadcast_in_dim x1, local copies, waits for them, and re-layouts, body(): jnp.broadcast_to(traces[None], (n_row, nc, rows))  0.74 us
  transfers between devices with their start and end apart: 1, of which 1 were waited for; matrix products, arithmetic and copies ran while one was open for 0% of the time, Pallas kernels for 0%

profile of v3, /device:TPU:0, one launch (start us, length us, event | category | flops | bytes accessed | tf_op | source)
XLA Modules:
  0.0 34.0 jit_solution(1489328927966349008)
XLA Ops:
  0.6 0.7 %broadcast_in_dim.2 = f32[16,8,512]{2,1,0:T(8,128)S(1)} broadcast(f32[8,512]{1,0:T(8,128)} %param.1), dimensions={1,2} | broadcast | bytes 278528 | tf_op jit(solution)/shard_map/broadcast_in_dim | solution.py:330
  1.4 18.0 %all_to_all.5.seen = f32[16,8,512]{2,1,0:T(8,128)S(1)} all-to-all(f32[16,8,512]{2,1,0:T(8,128)S(1)} %broadcast_in_dim.2), channel_id=1, replica_groups=mesh['row'=16,'col'=2] {'row'}, dimensions={0} | all-to-all | bytes 524288 | tf_op jit(solution)/shard_map/all_to_all | solution.py:330
  19.4 1.3 %collective-permute-start = (f32[16,1,512]{2,1,0:T(1,128)S(1)}, f32[16,1,512]{2,1,0:T(1,128)S(1)}, u32[]{:S(2)}, u32[]{:S(2)}) collective-permute-start(f32[16,1,512]{2,1,0:T(1,128)S(1)} %slice.4), channel_id=1, source_target_pairs={{0,1},{2,3},{4,5},{6,7},{8,9},{10,11},{12,13},{14,15},{16,17},{18,... | collective-permute-start | bytes 98312 | tf_op jit(solution)/shard_map/ppermute | solution.py:334
  20.7 0.8 %collective-permute-done.other = f32[16,1,512]{2,1,0:T(1,128)S(1)} collective-permute-done((f32[16,1,512]{2,1,0:T(1,128)S(1)}, f32[16,1,512]{2,1,0:T(1,128)S(1)}, u32[]{:S(2)}, u32[]{:S(2)}) %collective-permute-start) | collective-permute-done | bytes 32800 | tf_op jit(solution)/shard_map/ppermute | solution.py:334
  21.5 12.5 %shard_map.30 = (f32[512,2048]{1,0:T(8,128)}, f32[256,2048]{1,0:T(8,128)}) custom-call(f32[16,1,512]{2,1,0:T(1,128)S(1)} %collective-permute-done.other, f32[16,8,512]{2,1,0:T(8,128)S(1)} %all_to_all.5.seen), custom_call_target="tpu_custom_call" | custom-call | tf_op jit(solution)/shard_map/pallas_call | solution.py:299
  (1 shorter events, 0.0 us)
Async XLA Ops:
  19.4 2.1 %collective-permute-start = (f32[16,1,512]{2,1,0:T(1,128)S(1)}, f32[16,1,512]{2,1,0:T(1,128)S(1)}, u32[]{:S(2)}, u32[]{:S(2)}) collective-permute-start(f32[16,1,512]{2,1,0:T(1,128)S(1)} %slice.4), channel_id=1, source_target_pairs={{0,1},{2,3},{4,5},{6,7},{8,9},{10,11},{12,13},{14,15},{16,17},{18,... | collective-permute-start | bytes 98312 | tf_op jit(solution)/shard_map/ppermute | solution.py:334

commit v4 on v3

--- a/solution.py
+++ b/solution.py
@@ -12,7 +12,10 @@
 LANES = 128
 PANEL = 32
 SPAN = 16
-FIRST = True
+FIRST = False
+T = 0
+S = 2
+Q = 0
 F32 = jnp.float32
 BF16 = jnp.bfloat16
 LEFT = (0, 0, 1, 0, 2, 1)
@@ -55,12 +58,15 @@
         v = [{c: m[r0 + 8 * g : r0 + 8 * g + 8, LANES * c : LANES * (c + 1)] for c in tiles} for g in range(groups)]
         pivots = [None] * groups
         for s in range(0, groups, SPAN // 8):
+            pause(S)
             col = [[None] * groups for _ in range(SPAN)]
             for k in range(SPAN):
                 tile, lane = divmod(r0 + 8 * s + k, LANES)
                 for g in range(s + k // 8, groups):
                     col[k][g] = jnp.broadcast_to(v[g][tile][:, lane : lane + 1], (8, LANES))
             for j in range(0, SPAN, 2):
+                if j % 8 == 4:
+                    pause(Q)
                 p, i = s + j // 8, j % 8
                 x, y = col[j], col[j + 1]
                 pivot = [row_of(x[p], i), row_of(x[p], i + 1), row_of(y[p], i + 1)]
@@ -103,7 +109,7 @@
             for a in range(done // LANES, half):
                 left = joined(pieces[a], LEFT, 0)
                 updates += [(a, c, dot(left, right[c], TN)) for c in tiles if c >= a]
-            pause()
+            pause(T)
             for a, c, update in updates:
                 skip = max(0, done - LANES * a)
                 m[LANES * a + skip : LANES * (a + 1), LANES * c : LANES * (c + 1)] -= update[skip:, :]
@@ -233,33 +239,35 @@
     own = flip(lead[pl.ds(8 + start - tail, per + tail), :], turn)
     expand(in_row(own, reversed(range(per + tail))), 1 + TAPS, rows, window, 0, 0)
     own_rows = joined(split(window[0:rows, :], 2), LEFT[:SHORT], 1)
-    right = shifted(lead, blocks, -tail, (0, 1, 0, 1))
-    left = [joined(split(natural[pl.ds(c, blocks, stride=nc), :], 2), (0, 0, 1, 1), 0) for c in range(nc)]
+    right = shifted(lead, blocks, -tail, (0, 0, 1, 1))
+    left = [joined(split(natural[pl.ds(c, blocks, stride=nc), :], 2), (0, 1), 0) for c in range(nc)]
     left = dot(turn, jnp.concatenate(left, 0), NT).astype(BF16)
+    left = [left[:, 2 * blocks * c : 2 * blocks * (c + 1)] for c in range(nc)]
+    left = jnp.concatenate([jnp.concatenate([x, x], 1) for x in left], 0)
 
     def steps():
-        for c in range(nc):
-            products[c] = dot(left[:, 4 * blocks * c : 4 * blocks * (c + 1)], right)
+        for u in range(0, right.shape[1], 2 * LANES):
+            at = slice(u, min(u + 2 * LANES, right.shape[1]))
+            products[:, at] = dot(left, right[:, at])
+            yield
         for c in range(nc):
             last = [(per + tail + q) * nc + c for q in reversed(range(tail))]
             refs = (low_high.at[c], low_low.at[c])
             expand_split(jnp.concatenate([in_row(near, last), zeros], 1), 1 + TAPS, TAPS, refs)
-        yield
+            yield
         for c in range(nc):
-            expand(skewed_sum(products[c]), 1 + TAPS, TAPS, cross, 0, c * TAPS)
-            if c % 2 == 1:
-                yield
+            expand(skewed_sum(products[LANES * c : LANES * (c + 1), :]), 1 + TAPS, TAPS, cross, 0, c * TAPS)
+            yield
         for c in range(nc):
             at = slice(c * TAPS, (c + 1) * TAPS)
             whole = cross[:, at] + dot(tail_left, joined((low_high[c], low_low[c]), RIGHT[:SHORT], 0))
             cross_high[c], cross_low[c] = split(whole * scale, 2)
-            if c % 4 == 3:
-                yield
+            yield
 
     rest = steps()
     if FIRST:
         run(rest)
-    inverse_factor(gram, WIDE, lambda: next(rest, None))
+    inverse_factor(gram, WIDE, lambda n: [next(rest, None) for _ in range(n)])
     run(rest)
 
     pieces = split(gram[:, WIDE:], 2)
@@ -309,7 +317,7 @@
             pltpu.VMEM((blocks + 16, LANES), F32),
             pltpu.VMEM((WIDE, 2 * WIDE), F32),
             pltpu.VMEM((max(rows, TAPS), TAPS), F32),
-            pltpu.VMEM((nc, LANES, 2 * TAPS + LANES), F32),
+            pltpu.VMEM((nc * LANES, 2 * TAPS + LANES), F32),
             pltpu.VMEM((nc, TAPS, TAPS), BF16),
             pltpu.VMEM((nc, TAPS, TAPS), BF16),
             pltpu.VMEM((WIDE, nc * TAPS), F32),
@@ -331,7 +339,8 @@
     col = lax.axis_index("col")
     first, step = seen[:, 0:1], 1
     while step < n_col:
-        other = lax.ppermute(first, "col", [(i, i + step) for i in range(min(step, n_col - step))])
+        pairs = [(i, i ^ step) for i in range(n_col) if i ^ step < n_col]
+        other = lax.ppermute(first, "col", pairs)
         first, step = jnp.where(col < step, first, other), 2 * step
     return call((n_row, n_col, nc, rows), other, seen)
 

time: 34.3 us -> 33 us (0.962)
  starting transfers between devices: 1.29 us -> 0.07 us
  Pallas kernels: 12.5 us -> 12 us
  waiting for transfers between devices: 0.84 us -> 1.19 us
    ppermute x1, starting transfers between devices: 1.29 us -> 0.07 us  [body(): other = lax.ppermute(first, 'col', pairs)]
    pallas_call x1, Pallas kernels: 12.5 us -> 12 us  [call(): pl.pallas_call(functools.partial(kernel, sizes), out_shape=(jax.ShapeDtyp...]
    ppermute x1, waiting for transfers between devices: 0.84 us -> 1.19 us  [body(): other = lax.ppermute(first, 'col', pairs)]
where the time goes in v4:
time: 33 us; the launch traced here: 32.7 us
  blocking collectives  18 us (55%)
  Pallas kernels  12 us (36%)
  waiting for transfers between devices  1.19 us (4%)
  local copies, waits for them, and re-layouts  0.75 us (2%)
  between operations  0.65 us (2%)
    all_to_all x1, blocking collectives, body(): lax.all_to_all(jnp.broadcast_to(traces[None], (n_row, nc, rows)), 'row',...  18 us
    pallas_call x1, Pallas kernels, call(): pl.pallas_call(functools.partial(kernel, sizes), out_shape=(jax.ShapeDtyp...  12 us
    ppermute x1, waiting for transfers between devices, body(): other = lax.ppermute(first, 'col', pairs)  1.19 us
    broadcast_in_dim x1, local copies, waits for them, and re-layouts, body(): jnp.broadcast_to(traces[None], (n_row, nc, rows))  0.74 us
  transfers between devices with their start and end apart: 1, of which 1 were waited for; matrix products, arithmetic and copies ran while one was open for 0% of the time, Pallas kernels for 0%

profile of v4, /device:TPU:0, one launch (start us, length us, event | category | flops | bytes accessed | tf_op | source)
XLA Modules:
  0.0 32.7 jit_solution(13102290444201843083)
XLA Ops:
  0.6 0.7 %broadcast_in_dim.2 = f32[16,8,512]{2,1,0:T(8,128)S(1)} broadcast(f32[8,512]{1,0:T(8,128)} %param.1), dimensions={1,2} | broadcast | bytes 278528 | tf_op jit(solution)/shard_map/broadcast_in_dim | solution.py:338
  1.4 18.0 %all_to_all.5.seen = f32[16,8,512]{2,1,0:T(8,128)S(1)} all-to-all(f32[16,8,512]{2,1,0:T(8,128)S(1)} %broadcast_in_dim.2), channel_id=1, replica_groups=mesh['row'=16,'col'=2] {'row'}, dimensions={0} | all-to-all | bytes 524288 | tf_op jit(solution)/shard_map/all_to_all | solution.py:338
  19.4 0.1 collective-permute-start
  19.5 1.2 %collective-permute-done.other = f32[16,1,512]{2,1,0:T(1,128)S(1)} collective-permute-done((f32[16,1,512]{2,1,0:T(1,128)S(1)}, f32[16,1,512]{2,1,0:T(1,128)S(1)}, u32[]{:S(2)}, u32[]{:S(2)}) %collective-permute-start) | collective-permute-done | bytes 32800 | tf_op jit(solution)/shard_map/ppermute | solution.py:343
  20.6 12.0 %shard_map.30 = (f32[512,2048]{1,0:T(8,128)}, f32[256,2048]{1,0:T(8,128)}) custom-call(f32[16,1,512]{2,1,0:T(1,128)S(1)} %collective-permute-done.other, f32[16,8,512]{2,1,0:T(8,128)S(1)} %all_to_all.5.seen), custom_call_target="tpu_custom_call" | custom-call | tf_op jit(solution)/shard_map/pallas_call | solution.py:307
  (1 shorter events, 0.0 us)
Async XLA Ops:
  19.4 1.3 %collective-permute-start = (f32[16,1,512]{2,1,0:T(1,128)S(1)}, f32[16,1,512]{2,1,0:T(1,128)S(1)}, u32[]{:S(2)}, u32[]{:S(2)}) collective-permute-start(f32[16,1,512]{2,1,0:T(1,128)S(1)} %slice.4), channel_id=1, source_target_pairs={{0,1},{1,0},{2,3},{3,2},{4,5},{5,4},{6,7},{7,6},{8,9},{9,8},{10,11... | collective-permute-start | bytes 98312 | tf_op jit(solution)/shard_map/ppermute | solution.py:343
